TPU v7x, 512 devices: a whole 4x8x8 slice. The times are simulated.
512 devices in a mesh: box: 128 (over z, y, x_hi), seg: 4 (over x_lo, core).
Axes of the slice: x: 4 (x_hi: 2, x_lo: 2; x = x_hi * 2 + x_lo), y: 8, z: 8, core: 2. Of those that a mesh axis runs over, the one named last changes fastest.
Arguments:
- density_zero: bfloat16 [65536, 64], P('box'), may hold values from 0.25 to 4
- offsets: int32 [256, 4], P('box'), may hold values from -4 to 4, as said below
- start_one: int32 [128, 4, 1024], P('box', 'seg'), may hold values from 0 to 511, as said below
- slot_one: int32 [128, 4, 1024], P('box', 'seg'), may hold values from 0 to 3
- end_one: int32 [128, 4, 1024], P('box', 'seg'), may hold values from 0 to 255
- weight_one: float32 [128, 4, 1024], P('box', 'seg'), may hold values from 0.25 to 4
- start_two: int32 [128, 4, 1024], P('box', 'seg'), may hold values from 0 to 511, as said below
- slot_two: int32 [128, 4, 1024], P('box', 'seg'), may hold values from 0 to 3
- end_two: int32 [128, 4, 1024], P('box', 'seg'), may hold values from 0 to 255
- weight_two: float32 [128, 4, 1024], P('box', 'seg'), may hold values from 0.25 to 4
Outputs:
- density_one: bfloat16 [65536, 64], P('box')
- density_two: bfloat16 [65536, 64], P('box')
Inputs may be any that keep to these rules, and one draw needn't show every extreme that they name: `offsets`: in each row, the 4 entries are distinct. `start_one`: for every [g, l], each of the 512 rows appears exactly 1024 // 512 times. `start_two`: for every [g, l], each of the 512 rows appears exactly 1024 // 512 times.
All inputs are finite; a program needn't handle non-finite values.
Results may differ from a plain program's by a relative error of at most 0.009.
Values may be sent and summed in bfloat16 or wider, within the bound.
No kernel may reach another device: no remote copies, remote signals or barrier semaphores. Data moves between devices by JAX's collectives and lax.ppermute only.
A program may use at most 64 MiB of HBM per device.

v0:
```python
import jax
import jax.numpy as jnp
from jax import lax
from jax.sharding import PartitionSpec as P

REACH = 2


def from_behind(block, axis, distance):
    devices = range(lax.axis_size(axis))
    route = [((i - distance) % len(devices), i) for i in devices]
    return lax.ppermute(block, axis, route)


def three_parts(values):
    high = values.astype(jnp.bfloat16)
    rest = values - high.astype(jnp.float32)
    middle = rest.astype(jnp.bfloat16)
    low = (rest - middle.astype(jnp.float32)).astype(jnp.bfloat16)
    return (high, middle, low)


def onehot_left(table, values):
    total = None
    for member in three_parts(values):
        term = lax.dot_general(
            table, member, (((0,), (0,)), ((), ())), preferred_element_type=jnp.float32
        )
        total = term if total is None else total + term
    return total


def segment_pushes(start, slot, end, weight, scaled, width_k, block):
    rows, cols = scaled.shape
    blocks_dev = rows // block
    count = start.shape[0]
    step = min(2048, count)
    turns = count // step
    columns = blocks_dev * width_k * block

    def one_piece(acc, index):
        pick = (start[:, None] == jnp.arange(rows, dtype=jnp.int32)[None, :]).astype(jnp.bfloat16)
        fetched = jnp.dot(pick, scaled, preferred_element_type=jnp.float32)
        carried = fetched * weight[:, None]
        target = start // block * (width_k * block) + slot * block + end
        place = (target[:, None] == jnp.arange(columns, dtype=jnp.int32)[None, :]).astype(
            jnp.bfloat16
        )
        return (acc + onehot_left(place, carried), None)

    total, unused = lax.scan(one_piece, jnp.zeros((columns, cols), jnp.float32), jnp.arange(turns))
    return total.reshape(blocks_dev, width_k, block, cols)


def place_blocks(pushes, offsets):
    blocks_dev, width_k = offsets.shape
    span = 2 * REACH + 1
    target = jnp.arange(blocks_dev, dtype=jnp.int32)[:, None] + offsets + REACH * blocks_dev
    placing = (
        target[:, :, None] == jnp.arange(span * blocks_dev, dtype=jnp.int32)[None, None, :]
    ).astype(jnp.float32)
    return (placing, jnp.einsum("jku,jkec->uec", placing, pushes, precision=lax.Precision.HIGHEST))


def push_lanes(density, totals, start, slot, end, weight, offsets):
    rows, cols = density.shape
    blocks_dev, width_k = offsets.shape
    block = rows // blocks_dev
    span = 2 * REACH + 1
    scaled = (density.astype(jnp.float32) / totals[:, None]).astype(jnp.bfloat16)
    pushes = segment_pushes(start, slot, end, weight, scaled, width_k, block)
    placing, stacked = place_blocks(pushes, offsets)
    stacked = stacked.reshape(span, -1, 128)
    summed = lax.psum(stacked, "seg")
    combined = summed[REACH]
    for delta in range(-REACH, REACH + 1):
        if delta != 0:
            combined = combined + from_behind(summed[delta + REACH], "box", delta)
    return combined.reshape(rows, cols).astype(jnp.bfloat16)


def body(
    density_zero,
    offsets,
    start_one,
    slot_one,
    end_one,
    weight_one,
    start_two,
    slot_two,
    end_two,
    weight_two,
):
    rows = density_zero.shape[0]
    days = ((start_one, slot_one, end_one, weight_one), (start_two, slot_two, end_two, weight_two))
    flat = [tuple((member.reshape(-1) for member in day)) for day in days]
    density = density_zero
    results = []
    partial_totals = jnp.stack(
        [jax.ops.segment_sum(day[3], day[0], num_segments=rows) for day in flat]
    )
    totals = lax.psum(partial_totals, "seg")
    for number in range(2):
        starts, slots, ends, weights = flat[number]
        density = push_lanes(density, totals[number], starts, slots, ends, weights, offsets)
        results.append(density)
    return (results[0], results[1])


def solution(mesh):
    placed = (
        P("box", None),
        P("box", None),
        P("box", "seg", None),
        P("box", "seg", None),
        P("box", "seg", None),
        P("box", "seg", None),
        P("box", "seg", None),
        P("box", "seg", None),
        P("box", "seg", None),
        P("box", "seg", None),
    )
    return jax.shard_map(
        body,
        mesh=mesh,
        in_specs=placed,
        out_specs=(P("box", None), P("box", None)),
        check_vma=False,
    )
```

profile of v0, /device:TPU:1, one launch (start us, length us, event | category | flops | bytes accessed | tf_op | source)
XLA Modules:
  0.0 211.3 jit_solution(17053488340971013685)
XLA Ops:
  7.2 0.0 all-reduce.3.cloned.1.call-start
  7.2 0.7 add_add_fusion
  7.9 7.8 %scatter_custom_fusion = f32[512]{0:T(512)S(1)} fusion(s32[1024]{0:T(1024)} %bitcast.73, f32[1024]{0:T(1024)} %bitcast.82, f32[]{:T(128)} %constant.47.clone.1), kind=kCustom, calls=%fused_computation.91 | custom fusion | flops 1024 | bytes 2560 | tf_op jit(solution)/shard_map/scatter-add | solution.py:100
  15.7 7.8 %scatter_custom_fusion.1 = f32[512]{0:T(512)S(1)} fusion(s32[1024]{0:T(1024)} %bitcast.77, f32[1024]{0:T(1024)} %bitcast.84, f32[]{:T(128)} %constant.47.clone.1), kind=kCustom, calls=%fused_computation.89 | custom fusion | flops 1024 | bytes 2560 | tf_op jit(solution)/shard_map/scatter-add | solution.py:100
  23.4 11.9 %psum.21 = f32[2,512]{1,0:T(2,128)S(1)} all-reduce(f32[2,512]{1,0:T(2,128)S(1)} %pad_maximum_fusion), channel_id=1, replica_groups=mesh['box'=128,'seg'=4] {'seg'}, use_global_device_ids=true, to_apply=%region_2.0 | all-reduce | flops 1024 | bytes 8192 | tf_op jit(solution)/shard_map/psum | solution.py:102
  35.3 0.7 broadcast_multiply_fusion.1
  36.0 0.7 fusion.43
  36.7 1.5 fusion.19
  38.2 1.8 fusion.4
  40.0 1.6 fusion.12
  41.6 1.8 fusion.13
  43.4 0.4 reshape.136
  43.7 0.7 convolution_bitcast_fusion.1
  44.5 0.5 copy.12
  45.0 1.1 reshape.137
  46.1 0.0 all-reduce.3.cloned.1.call-update
  46.1 0.0 all-reduce.5.cloned.1.call-start
  46.2 50.1 %all-reduce.3.cloned.1.call-done = f32[5,256,128]{2,1,0:T(8,128)} async-done(((f32[5,256,128]{2,1,0:T(8,128)}), f32[5,256,128]{2,1,0:T(8,128)}) %all-reduce.3.cloned.1.call-update) | async-done | bytes 655376 | tf_op jit(solution)/shard_map/psum | solution.py:74
  96.3 1.1 slice_bitcast_fusion.8
  97.4 7.5 %collective-permute-start = (f32[256,128]{1,0:T(8,128)S(1)}, f32[256,128]{1,0:T(8,128)S(1)}, u32[]{:S(2)}, u32[]{:S(2)}) collective-permute-start(f32[256,128]{1,0:T(8,128)S(1)} %get-tuple-element.48), channel_id=1, source_target_pairs={{8,0},{12,4},{16,8},{20,12},{24,16},{28,20},{32,24},{36,28},{40,32... | collective-permute-start | bytes 393224 | tf_op jit(solution)/shard_map/ppermute | solution.py:12
  105.0 1.9 collective-permute-start.3
  106.9 4.3 %collective-permute-start.2 = (f32[256,128]{1,0:T(8,128)S(1)}, f32[256,128]{1,0:T(8,128)S(1)}, u32[]{:S(2)}, u32[]{:S(2)}) collective-permute-start(f32[256,128]{1,0:T(8,128)S(1)} %get-tuple-element.50), channel_id=1, source_target_pairs={{508,0},{0,4},{4,8},{8,12},{12,16},{16,20},{20,24},{24,28},{28,32}... | collective-permute-start | bytes 393224 | tf_op jit(solution)/shard_map/ppermute | solution.py:12
  111.2 6.9 %collective-permute-start.1 = (f32[256,128]{1,0:T(8,128)S(1)}, f32[256,128]{1,0:T(8,128)S(1)}, u32[]{:S(2)}, u32[]{:S(2)}) collective-permute-start(f32[256,128]{1,0:T(8,128)S(1)} %get-tuple-element.51), channel_id=1, source_target_pairs={{4,0},{8,4},{12,8},{16,12},{20,16},{24,20},{28,24},{32,28},{36,32}... | collective-permute-start | bytes 393224 | tf_op jit(solution)/shard_map/ppermute | solution.py:12
  118.2 1.9 collective-permute-done.2
  120.1 2.2 %collective-permute-done.1 = f32[256,128]{1,0:T(8,128)S(1)} collective-permute-done((f32[256,128]{1,0:T(8,128)S(1)}, f32[256,128]{1,0:T(8,128)S(1)}, u32[]{:S(2)}, u32[]{:S(2)}) %collective-permute-start.1) | collective-permute-done | bytes 131104 | tf_op jit(solution)/shard_map/ppermute | solution.py:12
  122.3 1.0 fusion.37
  123.2 0.1 convert_element_type.82
  123.3 0.7 fusion.18
  124.0 1.8 fusion.1
  125.8 1.6 fusion.14
  127.4 1.8 fusion.15
  129.2 0.4 reshape.139
  129.5 0.7 convolution_bitcast_fusion
  130.3 0.5 copy.13
  130.8 1.1 reshape.140
  131.9 0.0 all-reduce.5.cloned.1.call-update
  131.9 44.8 %all-reduce.5.cloned.1.call-done = f32[5,256,128]{2,1,0:T(8,128)} async-done(((f32[5,256,128]{2,1,0:T(8,128)}), f32[5,256,128]{2,1,0:T(8,128)}) %all-reduce.5.cloned.1.call-update) | async-done | bytes 655376 | tf_op jit(solution)/shard_map/psum | solution.py:74
  176.7 1.1 slice_bitcast_fusion.3
  177.9 7.5 %collective-permute-start.4 = (f32[256,128]{1,0:T(8,128)S(1)}, f32[256,128]{1,0:T(8,128)S(1)}, u32[]{:S(2)}, u32[]{:S(2)}) collective-permute-start(f32[256,128]{1,0:T(8,128)S(1)} %get-tuple-element.36), channel_id=1, source_target_pairs={{8,0},{12,4},{16,8},{20,12},{24,16},{28,20},{32,24},{36,28},{40,32... | collective-permute-start | bytes 393224 | tf_op jit(solution)/shard_map/ppermute | solution.py:12
  185.4 1.9 collective-permute-start.7
  187.3 4.3 %collective-permute-start.6 = (f32[256,128]{1,0:T(8,128)S(1)}, f32[256,128]{1,0:T(8,128)S(1)}, u32[]{:S(2)}, u32[]{:S(2)}) collective-permute-start(f32[256,128]{1,0:T(8,128)S(1)} %get-tuple-element.38), channel_id=1, source_target_pairs={{508,0},{0,4},{4,8},{8,12},{12,16},{16,20},{20,24},{24,28},{28,32}... | collective-permute-start | bytes 393224 | tf_op jit(solution)/shard_map/ppermute | solution.py:12
  191.7 6.7 %collective-permute-start.5 = (f32[256,128]{1,0:T(8,128)S(1)}, f32[256,128]{1,0:T(8,128)S(1)}, u32[]{:S(2)}, u32[]{:S(2)}) collective-permute-start(f32[256,128]{1,0:T(8,128)S(1)} %get-tuple-element.39), channel_id=1, source_target_pairs={{4,0},{8,4},{12,8},{16,12},{20,16},{24,20},{28,24},{32,28},{36,32}... | collective-permute-start | bytes 393224 | tf_op jit(solution)/shard_map/ppermute | solution.py:12
  198.4 0.7 copy.14
  199.1 1.4 collective-permute-done.6
  200.5 2.2 %collective-permute-done.5 = f32[256,128]{1,0:T(8,128)S(1)} collective-permute-done((f32[256,128]{1,0:T(8,128)S(1)}, f32[256,128]{1,0:T(8,128)S(1)}, u32[]{:S(2)}, u32[]{:S(2)}) %collective-permute-start.5) | collective-permute-done | bytes 131104 | tf_op jit(solution)/shard_map/ppermute | solution.py:12
  202.7 0.9 fusion.32
  203.6 0.1 convert_element_type.91
  203.7 0.7 copy.15
  (16 shorter events, 0.1 us)
Async XLA Ops:
  7.2 89.1 %all-reduce.3.cloned.1.call-start = ((), (), s32[]{:S(2)}) async-start(), calls=%async_computation | async-start | bytes 1310720 | tf_op jit(solution)/shard_map/psum | solution.py:74
  45.0 1.2 copy-start
  46.1 72.0 %copy-start.1 = (s32[1,1,1024]{2,1,0:T(1,128)S(1)}, s32[1,1,1024]{2,1,0:T(1,128)}, u32[]{:S(2)}) copy-start(s32[1,1,1024]{2,1,0:T(1,128)} %param.18) | copy-start | bytes 12292
  46.1 72.0 %copy-start.2 = (s32[1,1,1024]{2,1,0:T(1,128)S(1)}, s32[1,1,1024]{2,1,0:T(1,128)}, u32[]{:S(2)}) copy-start(s32[1,1,1024]{2,1,0:T(1,128)} %param.16) | copy-start | bytes 12292
  46.1 77.2 %copy-start.3 = (f32[1,1,1024]{2,1,0:T(1,128)S(1)}, f32[1,1,1024]{2,1,0:T(1,128)}, u32[]{:S(2)}) copy-start(f32[1,1,1024]{2,1,0:T(1,128)} %param.19) | copy-start | bytes 12292
  46.1 130.6 %all-reduce.5.cloned.1.call-start = ((), (), s32[]{:S(2)}) async-start(), calls=%async_computation.1 | async-start | bytes 1310720 | tf_op jit(solution)/shard_map/psum | solution.py:74
  97.4 20.7 %collective-permute-start = (f32[256,128]{1,0:T(8,128)S(1)}, f32[256,128]{1,0:T(8,128)S(1)}, u32[]{:S(2)}, u32[]{:S(2)}) collective-permute-start(f32[256,128]{1,0:T(8,128)S(1)} %get-tuple-element.48), channel_id=1, source_target_pairs={{8,0},{12,4},{16,8},{20,12},{24,16},{28,20},{32,24},{36,28},{40,32... | collective-permute-start | bytes 393224 | tf_op jit(solution)/shard_map/ppermute | solution.py:12
  105.0 13.2 %collective-permute-start.3 = (f32[256,128]{1,0:T(8,128)S(1)}, f32[256,128]{1,0:T(8,128)S(1)}, u32[]{:S(2)}, u32[]{:S(2)}) collective-permute-start(f32[256,128]{1,0:T(8,128)S(1)} %get-tuple-element.49), channel_id=1, source_target_pairs={{504,0},{508,4},{0,8},{4,12},{8,16},{12,20},{16,24},{20,28},{24,32... | collective-permute-start | bytes 393224 | tf_op jit(solution)/shard_map/ppermute | solution.py:12
  106.9 13.2 %collective-permute-start.2 = (f32[256,128]{1,0:T(8,128)S(1)}, f32[256,128]{1,0:T(8,128)S(1)}, u32[]{:S(2)}, u32[]{:S(2)}) collective-permute-start(f32[256,128]{1,0:T(8,128)S(1)} %get-tuple-element.50), channel_id=1, source_target_pairs={{508,0},{0,4},{4,8},{8,12},{12,16},{16,20},{20,24},{24,28},{28,32}... | collective-permute-start | bytes 393224 | tf_op jit(solution)/shard_map/ppermute | solution.py:12
  111.2 11.0 %collective-permute-start.1 = (f32[256,128]{1,0:T(8,128)S(1)}, f32[256,128]{1,0:T(8,128)S(1)}, u32[]{:S(2)}, u32[]{:S(2)}) collective-permute-start(f32[256,128]{1,0:T(8,128)S(1)} %get-tuple-element.51), channel_id=1, source_target_pairs={{4,0},{8,4},{12,8},{16,12},{20,16},{24,20},{28,24},{32,28},{36,32}... | collective-permute-start | bytes 393224 | tf_op jit(solution)/shard_map/ppermute | solution.py:12
  177.9 21.2 %collective-permute-start.4 = (f32[256,128]{1,0:T(8,128)S(1)}, f32[256,128]{1,0:T(8,128)S(1)}, u32[]{:S(2)}, u32[]{:S(2)}) collective-permute-start(f32[256,128]{1,0:T(8,128)S(1)} %get-tuple-element.36), channel_id=1, source_target_pairs={{8,0},{12,4},{16,8},{20,12},{24,16},{28,20},{32,24},{36,28},{40,32... | collective-permute-start | bytes 393224 | tf_op jit(solution)/shard_map/ppermute | solution.py:12
  185.4 13.7 %collective-permute-start.7 = (f32[256,128]{1,0:T(8,128)S(1)}, f32[256,128]{1,0:T(8,128)S(1)}, u32[]{:S(2)}, u32[]{:S(2)}) collective-permute-start(f32[256,128]{1,0:T(8,128)S(1)} %get-tuple-element.37), channel_id=1, source_target_pairs={{504,0},{508,4},{0,8},{4,12},{8,16},{12,20},{16,24},{20,28},{24,32... | collective-permute-start | bytes 393224 | tf_op jit(solution)/shard_map/ppermute | solution.py:12
  187.3 13.2 %collective-permute-start.6 = (f32[256,128]{1,0:T(8,128)S(1)}, f32[256,128]{1,0:T(8,128)S(1)}, u32[]{:S(2)}, u32[]{:S(2)}) collective-permute-start(f32[256,128]{1,0:T(8,128)S(1)} %get-tuple-element.38), channel_id=1, source_target_pairs={{508,0},{0,4},{4,8},{8,12},{12,16},{16,20},{20,24},{24,28},{28,32}... | collective-permute-start | bytes 393224 | tf_op jit(solution)/shard_map/ppermute | solution.py:12
  191.7 11.0 %collective-permute-start.5 = (f32[256,128]{1,0:T(8,128)S(1)}, f32[256,128]{1,0:T(8,128)S(1)}, u32[]{:S(2)}, u32[]{:S(2)}) collective-permute-start(f32[256,128]{1,0:T(8,128)S(1)} %get-tuple-element.39), channel_id=1, source_target_pairs={{4,0},{8,4},{12,8},{16,12},{20,16},{24,20},{28,24},{32,28},{36,32}... | collective-permute-start | bytes 393224 | tf_op jit(solution)/shard_map/ppermute | solution.py:12
Sparse Core Ops, SparseCore 0:
  46.2 50.0 all-reduce.2
  132.0 44.6 all-reduce.4
where the time goes:
time: 212 us; the launch traced here: 211 us
  waiting for transfers between devices  103 us (49%)
  starting transfers between devices  41.2 us (19%)
  other arithmetic  19.5 us (9%)
  between operations  14.3 us (7%)
  matrix products  13.9 us (7%)
  blocking collectives  11.9 us (6%)
  local copies, waits for them, and re-layouts  7.8 us (4%)
    psum x2, waiting for transfers between devices, push_lanes(): summed = lax.psum(stacked, 'seg')  95 us
    ppermute x8, starting transfers between devices, from_behind(): return lax.ppermute(block, axis, route)  41.1 us
    scatter-add x2, other arithmetic, body(): jax.ops.segment_sum(day[3], day[0], num_segments=rows)  15.5 us
    psum x1, blocking collectives, body(): totals = lax.psum(partial_totals, 'seg')  11.9 us
    dot_general x6, matrix products, onehot_left(): lax.dot_general(table, member, (((0,), (0,)), ((), ())), preferred_elemen...  10.3 us
    ppermute x8, waiting for transfers between devices, from_behind(): return lax.ppermute(block, axis, route)  7.71 us
  transfers between devices with their start and end apart: 10, of which 6 were waited for; matrix products, arithmetic and copies ran while one was open for 0% of the time, Pallas kernels for 0%

commit v1 on v0

--- a/solution.py
+++ b/solution.py
@@ -1,9 +1,19 @@
+import functools
 import jax
 import jax.numpy as jnp
 from jax import lax
 from jax.sharding import PartitionSpec as P
 
 REACH = 2
+
+
+def grid_pass(patch, along_axis):
+    local_out = lax.all_gather(patch, along_axis)
+    s_next = jnp.sum(local_out, 0)
+    return s_next
+
+
+launch_the_thing = functools.partial(grid_pass, along_axis="seg")
 
 
 def from_behind(block, axis, distance):
@@ -71,7 +81,7 @@
     pushes = segment_pushes(start, slot, end, weight, scaled, width_k, block)
     placing, stacked = place_blocks(pushes, offsets)
     stacked = stacked.reshape(span, -1, 128)
-    summed = lax.psum(stacked, "seg")
+    summed = launch_the_thing(stacked)
     combined = summed[REACH]
     for delta in range(-REACH, REACH + 1):
         if delta != 0:

time: 212 us -> 191 us (0.901)
  waiting for transfers between devices: 103 us -> 81.5 us
  local copies, waits for them, and re-layouts: 7.8 us -> 5.62 us
    psum x2 -> x0, waiting for transfers between devices: 95 us -> none  [push_lanes(): summed = lax.psum(stacked, 'seg')]
    all_gather x0 -> x2, waiting for transfers between devices: none -> 73.4 us  [grid_pass(): local_out = lax.all_gather(patch, along_axis)]
    reduce_sum x0 -> x2, other arithmetic: none -> 3.91 us  [grid_pass(): s_next = jnp.sum(local_out, 0)]
    squeeze x2, local copies, waits for them, and re-layouts: 2.26 us -> 0.07 us  [push_lanes(): combined = combined + from_behind(summed[delta + REACH], 'box', delta)]
    reshape x2 -> x0, local copies, waits for them, and re-layouts: 2.18 us -> none  [push_lanes(): stacked = stacked.reshape(span, -1, 128)]
    another operation x0 -> x2, local copies, waits for them, and re-layouts: none -> 2.17 us  [grid_pass(): local_out = lax.all_gather(patch, along_axis)]
where the time goes in v1:
time: 191 us
  waiting for transfers between devices  81.5 us (43%)
  starting transfers between devices  41.8 us (22%)
  other arithmetic  21.6 us (11%)
  between operations  14.3 us (7%)
  matrix products  13.9 us (7%)
  blocking collectives  11.9 us (6%)
  local copies, waits for them, and re-layouts  5.62 us (3%)
    all_gather x2, waiting for transfers between devices, grid_pass(): local_out = lax.all_gather(patch, along_axis)  73.4 us
    ppermute x8, starting transfers between devices, from_behind(): return lax.ppermute(block, axis, route)  41.7 us
    scatter-add x2, other arithmetic, body(): jax.ops.segment_sum(day[3], day[0], num_segments=rows)  15.5 us
    psum x1, blocking collectives, body(): totals = lax.psum(partial_totals, 'seg')  11.9 us
    dot_general x6, matrix products, onehot_left(): lax.dot_general(table, member, (((0,), (0,)), ((), ())), preferred_elemen...  10.3 us
    ppermute x8, waiting for transfers between devices, from_behind(): return lax.ppermute(block, axis, route)  8.03 us
    reduce_sum x2, other arithmetic, grid_pass(): s_next = jnp.sum(local_out, 0)  3.91 us
  transfers between devices with their start and end apart: 10, of which 6 were waited for; matrix products, arithmetic and copies ran while one was open for 0% of the time, Pallas kernels for 0%

profile of v1, /device:TPU:1, one launch (start us, length us, event | category | flops | bytes accessed | tf_op | source)
XLA Modules:
  0.0 190.7 jit_solution(5222708920339940392)
XLA Ops:
  7.2 0.0 all-gather.3.cloned.1.call-start
  7.2 0.7 add_add_fusion
  7.9 7.8 %scatter_custom_fusion = f32[512]{0:T(512)S(1)} fusion(s32[1024]{0:T(1024)} %bitcast.73, f32[1024]{0:T(1024)} %bitcast.82, f32[]{:T(128)} %constant.48.clone.1), kind=kCustom, calls=%fused_computation.91 | custom fusion | flops 1024 | bytes 2560 | tf_op jit(solution)/shard_map/scatter-add | solution.py:110
  15.7 7.8 %scatter_custom_fusion.1 = f32[512]{0:T(512)S(1)} fusion(s32[1024]{0:T(1024)} %bitcast.77, f32[1024]{0:T(1024)} %bitcast.84, f32[]{:T(128)} %constant.48.clone.1), kind=kCustom, calls=%fused_computation.89 | custom fusion | flops 1024 | bytes 2560 | tf_op jit(solution)/shard_map/scatter-add | solution.py:110
  23.4 11.9 %psum.7 = f32[2,512]{1,0:T(2,128)S(1)} all-reduce(f32[2,512]{1,0:T(2,128)S(1)} %pad_maximum_fusion), channel_id=1, replica_groups=mesh['box'=128,'seg'=4] {'seg'}, use_global_device_ids=true, to_apply=%region_2.0 | all-reduce | flops 1024 | bytes 8192 | tf_op jit(solution)/shard_map/psum | solution.py:112
  35.3 0.7 broadcast_multiply_fusion.1
  36.0 0.7 fusion.43
  36.7 1.5 fusion.19
  38.2 1.8 fusion.4
  40.0 1.6 fusion.12
  41.6 1.8 fusion.13
  43.4 0.4 reshape.130
  43.7 0.7 convolution_bitcast_fusion.1
  44.5 0.0 copy-start
  44.5 0.5 copy.16
  45.0 1.1 all_gather_reshape.6
  46.1 0.0 all-gather.3.cloned.1.call-update
  46.1 0.0 all-gather.5.cloned.1.call-start
  46.2 0.0 copy-start.1
  46.2 39.5 %all-gather.3.cloned.1.call-done = f32[4,5,256,128]{3,2,1,0:T(8,128)} async-done(((f32[1,5,256,128]{3,2,1,0:T(8,128)}), f32[4,5,256,128]{3,2,1,0:T(8,128)}) %all-gather.3.cloned.1.call-update) | async-done | bytes 2621456 | tf_op jit(solution)/shard_map/all_gather | solution.py:11
  85.7 2.0 %reduce_sum.18 = f32[5,256,128]{2,1,0:T(8,128)S(1)} reduce(f32[4,5,256,128]{3,2,1,0:T(8,128)} %all-gather.3.cloned.1.call-done, f32[]{:T(128)} %constant.48.clone.1), dimensions={0}, to_apply=%region_3.4 | reduce | flops 491520 | bytes 3276804 | tf_op jit(solution)/shard_map/reduce_sum | solution.py:12
  87.7 7.9 %collective-permute-start = (f32[256,128]{1,0:T(8,128)S(1)}, f32[256,128]{1,0:T(8,128)S(1)}, u32[]{:S(2)}, u32[]{:S(2)}) collective-permute-start(f32[256,128]{1,0:T(8,128)S(1)} %get-tuple-element.50), channel_id=1, source_target_pairs={{8,0},{12,4},{16,8},{20,12},{24,16},{28,20},{32,24},{36,28},{40,32... | collective-permute-start | bytes 393224 | tf_op jit(solution)/shard_map/ppermute | solution.py:22
  95.5 1.9 %collective-permute-start.3 = (f32[256,128]{1,0:T(8,128)S(1)}, f32[256,128]{1,0:T(8,128)S(1)}, u32[]{:S(2)}, u32[]{:S(2)}) collective-permute-start(f32[256,128]{1,0:T(8,128)S(1)} %get-tuple-element.51), channel_id=1, source_target_pairs={{504,0},{508,4},{0,8},{4,12},{8,16},{12,20},{16,24},{20,28},{24,32... | collective-permute-start | bytes 393224 | tf_op jit(solution)/shard_map/ppermute | solution.py:22
  97.5 4.3 %collective-permute-start.2 = (f32[256,128]{1,0:T(8,128)S(1)}, f32[256,128]{1,0:T(8,128)S(1)}, u32[]{:S(2)}, u32[]{:S(2)}) collective-permute-start(f32[256,128]{1,0:T(8,128)S(1)} %get-tuple-element.52), channel_id=1, source_target_pairs={{508,0},{0,4},{4,8},{8,12},{12,16},{16,20},{20,24},{24,28},{28,32}... | collective-permute-start | bytes 393224 | tf_op jit(solution)/shard_map/ppermute | solution.py:22
  101.8 6.9 %collective-permute-start.1 = (f32[256,128]{1,0:T(8,128)S(1)}, f32[256,128]{1,0:T(8,128)S(1)}, u32[]{:S(2)}, u32[]{:S(2)}) collective-permute-start(f32[256,128]{1,0:T(8,128)S(1)} %get-tuple-element.53), channel_id=1, source_target_pairs={{4,0},{8,4},{12,8},{16,12},{20,16},{24,20},{28,24},{32,28},{36,32}... | collective-permute-start | bytes 393224 | tf_op jit(solution)/shard_map/ppermute | solution.py:22
  108.7 1.9 %collective-permute-done.2 = f32[256,128]{1,0:T(8,128)S(1)} collective-permute-done((f32[256,128]{1,0:T(8,128)S(1)}, f32[256,128]{1,0:T(8,128)S(1)}, u32[]{:S(2)}, u32[]{:S(2)}) %collective-permute-start.2) | collective-permute-done | bytes 131104 | tf_op jit(solution)/shard_map/ppermute | solution.py:22
  110.7 2.3 %collective-permute-done.1 = f32[256,128]{1,0:T(8,128)S(1)} collective-permute-done((f32[256,128]{1,0:T(8,128)S(1)}, f32[256,128]{1,0:T(8,128)S(1)}, u32[]{:S(2)}, u32[]{:S(2)}) %collective-permute-start.1) | collective-permute-done | bytes 131104 | tf_op jit(solution)/shard_map/ppermute | solution.py:22
  113.0 0.1 convert_element_type.82
  113.1 0.7 fusion.18
  113.8 1.8 fusion.1
  115.6 1.6 fusion.14
  117.2 1.8 fusion.15
  119.0 0.4 reshape.132
  119.4 0.7 convolution_bitcast_fusion
  120.1 0.5 copy.17
  120.6 1.1 all_gather_reshape.7
  121.7 0.0 all-gather.5.cloned.1.call-update
  121.7 34.0 %all-gather.5.cloned.1.call-done = f32[4,5,256,128]{3,2,1,0:T(8,128)} async-done(((f32[1,5,256,128]{3,2,1,0:T(8,128)}), f32[4,5,256,128]{3,2,1,0:T(8,128)}) %all-gather.5.cloned.1.call-update) | async-done | bytes 2621456 | tf_op jit(solution)/shard_map/all_gather | solution.py:11
  155.7 2.0 %reduce_sum.19 = f32[5,256,128]{2,1,0:T(8,128)S(1)} reduce(f32[4,5,256,128]{3,2,1,0:T(8,128)} %all-gather.5.cloned.1.call-done, f32[]{:T(128)} %constant.48.clone.1), dimensions={0}, to_apply=%region_4.5 | reduce | flops 491520 | bytes 3276804 | tf_op jit(solution)/shard_map/reduce_sum | solution.py:12
  157.7 7.9 %collective-permute-start.4 = (f32[256,128]{1,0:T(8,128)S(1)}, f32[256,128]{1,0:T(8,128)S(1)}, u32[]{:S(2)}, u32[]{:S(2)}) collective-permute-start(f32[256,128]{1,0:T(8,128)S(1)} %get-tuple-element.38), channel_id=1, source_target_pairs={{8,0},{12,4},{16,8},{20,12},{24,16},{28,20},{32,24},{36,28},{40,32... | collective-permute-start | bytes 393224 | tf_op jit(solution)/shard_map/ppermute | solution.py:22
  165.6 1.9 %collective-permute-start.7 = (f32[256,128]{1,0:T(8,128)S(1)}, f32[256,128]{1,0:T(8,128)S(1)}, u32[]{:S(2)}, u32[]{:S(2)}) collective-permute-start(f32[256,128]{1,0:T(8,128)S(1)} %get-tuple-element.39), channel_id=1, source_target_pairs={{504,0},{508,4},{0,8},{4,12},{8,16},{12,20},{16,24},{20,28},{24,32... | collective-permute-start | bytes 393224 | tf_op jit(solution)/shard_map/ppermute | solution.py:22
  167.5 4.3 %collective-permute-start.6 = (f32[256,128]{1,0:T(8,128)S(1)}, f32[256,128]{1,0:T(8,128)S(1)}, u32[]{:S(2)}, u32[]{:S(2)}) collective-permute-start(f32[256,128]{1,0:T(8,128)S(1)} %get-tuple-element.48), channel_id=1, source_target_pairs={{508,0},{0,4},{4,8},{8,12},{12,16},{16,20},{20,24},{24,28},{28,32}... | collective-permute-start | bytes 393224 | tf_op jit(solution)/shard_map/ppermute | solution.py:22
  171.8 6.7 %collective-permute-start.5 = (f32[256,128]{1,0:T(8,128)S(1)}, f32[256,128]{1,0:T(8,128)S(1)}, u32[]{:S(2)}, u32[]{:S(2)}) collective-permute-start(f32[256,128]{1,0:T(8,128)S(1)} %get-tuple-element.49), channel_id=1, source_target_pairs={{4,0},{8,4},{12,8},{16,12},{20,16},{24,20},{28,24},{32,28},{36,32}... | collective-permute-start | bytes 393224 | tf_op jit(solution)/shard_map/ppermute | solution.py:22
  178.5 0.7 copy.18
  179.2 1.4 collective-permute-done.6
  180.7 2.3 %collective-permute-done.5 = f32[256,128]{1,0:T(8,128)S(1)} collective-permute-done((f32[256,128]{1,0:T(8,128)S(1)}, f32[256,128]{1,0:T(8,128)S(1)}, u32[]{:S(2)}, u32[]{:S(2)}) %collective-permute-start.5) | collective-permute-done | bytes 131104 | tf_op jit(solution)/shard_map/ppermute | solution.py:22
  183.0 0.1 convert_element_type.91
  183.1 0.7 copy.19
  (18 shorter events, 0.2 us)
Async XLA Ops:
  7.2 78.5 %all-gather.3.cloned.1.call-start = ((), (), s32[]{:S(2)}) async-start(), calls=%async_computation | async-start | bytes 3276800 | tf_op jit(solution)/shard_map/all_gather | solution.py:11
  44.5 1.7 copy-start
  46.1 109.6 %all-gather.5.cloned.1.call-start = ((), (), s32[]{:S(2)}) async-start(), calls=%async_computation.1 | async-start | bytes 3276800 | tf_op jit(solution)/shard_map/all_gather | solution.py:11
  46.2 62.5 %copy-start.1 = (s32[1,1,1024]{2,1,0:T(1,128)S(1)}, s32[1,1,1024]{2,1,0:T(1,128)}, u32[]{:S(2)}) copy-start(s32[1,1,1024]{2,1,0:T(1,128)} %param.18) | copy-start | bytes 12292
  46.2 62.5 %copy-start.2 = (s32[1,1,1024]{2,1,0:T(1,128)S(1)}, s32[1,1,1024]{2,1,0:T(1,128)}, u32[]{:S(2)}) copy-start(s32[1,1,1024]{2,1,0:T(1,128)} %param.16) | copy-start | bytes 12292
  46.2 66.9 %copy-start.3 = (f32[1,1,1024]{2,1,0:T(1,128)S(1)}, f32[1,1,1024]{2,1,0:T(1,128)}, u32[]{:S(2)}) copy-start(f32[1,1,1024]{2,1,0:T(1,128)} %param.19) | copy-start | bytes 12292
  87.7 21.0 %collective-permute-start = (f32[256,128]{1,0:T(8,128)S(1)}, f32[256,128]{1,0:T(8,128)S(1)}, u32[]{:S(2)}, u32[]{:S(2)}) collective-permute-start(f32[256,128]{1,0:T(8,128)S(1)} %get-tuple-element.50), channel_id=1, source_target_pairs={{8,0},{12,4},{16,8},{20,12},{24,16},{28,20},{32,24},{36,28},{40,32... | collective-permute-start | bytes 393224 | tf_op jit(solution)/shard_map/ppermute | solution.py:22
  95.5 13.2 %collective-permute-start.3 = (f32[256,128]{1,0:T(8,128)S(1)}, f32[256,128]{1,0:T(8,128)S(1)}, u32[]{:S(2)}, u32[]{:S(2)}) collective-permute-start(f32[256,128]{1,0:T(8,128)S(1)} %get-tuple-element.51), channel_id=1, source_target_pairs={{504,0},{508,4},{0,8},{4,12},{8,16},{12,20},{16,24},{20,28},{24,32... | collective-permute-start | bytes 393224 | tf_op jit(solution)/shard_map/ppermute | solution.py:22
  97.5 13.2 %collective-permute-start.2 = (f32[256,128]{1,0:T(8,128)S(1)}, f32[256,128]{1,0:T(8,128)S(1)}, u32[]{:S(2)}, u32[]{:S(2)}) collective-permute-start(f32[256,128]{1,0:T(8,128)S(1)} %get-tuple-element.52), channel_id=1, source_target_pairs={{508,0},{0,4},{4,8},{8,12},{12,16},{16,20},{20,24},{24,28},{28,32}... | collective-permute-start | bytes 393224 | tf_op jit(solution)/shard_map/ppermute | solution.py:22
  101.8 11.2 %collective-permute-start.1 = (f32[256,128]{1,0:T(8,128)S(1)}, f32[256,128]{1,0:T(8,128)S(1)}, u32[]{:S(2)}, u32[]{:S(2)}) collective-permute-start(f32[256,128]{1,0:T(8,128)S(1)} %get-tuple-element.53), channel_id=1, source_target_pairs={{4,0},{8,4},{12,8},{16,12},{20,16},{24,20},{28,24},{32,28},{36,32}... | collective-permute-start | bytes 393224 | tf_op jit(solution)/shard_map/ppermute | solution.py:22
  157.7 21.5 %collective-permute-start.4 = (f32[256,128]{1,0:T(8,128)S(1)}, f32[256,128]{1,0:T(8,128)S(1)}, u32[]{:S(2)}, u32[]{:S(2)}) collective-permute-start(f32[256,128]{1,0:T(8,128)S(1)} %get-tuple-element.38), channel_id=1, source_target_pairs={{8,0},{12,4},{16,8},{20,12},{24,16},{28,20},{32,24},{36,28},{40,32... | collective-permute-start | bytes 393224 | tf_op jit(solution)/shard_map/ppermute | solution.py:22
  165.6 13.7 %collective-permute-start.7 = (f32[256,128]{1,0:T(8,128)S(1)}, f32[256,128]{1,0:T(8,128)S(1)}, u32[]{:S(2)}, u32[]{:S(2)}) collective-permute-start(f32[256,128]{1,0:T(8,128)S(1)} %get-tuple-element.39), channel_id=1, source_target_pairs={{504,0},{508,4},{0,8},{4,12},{8,16},{12,20},{16,24},{20,28},{24,32... | collective-permute-start | bytes 393224 | tf_op jit(solution)/shard_map/ppermute | solution.py:22
  167.5 13.2 %collective-permute-start.6 = (f32[256,128]{1,0:T(8,128)S(1)}, f32[256,128]{1,0:T(8,128)S(1)}, u32[]{:S(2)}, u32[]{:S(2)}) collective-permute-start(f32[256,128]{1,0:T(8,128)S(1)} %get-tuple-element.48), channel_id=1, source_target_pairs={{508,0},{0,4},{4,8},{8,12},{12,16},{16,20},{20,24},{24,28},{28,32}... | collective-permute-start | bytes 393224 | tf_op jit(solution)/shard_map/ppermute | solution.py:22
  171.8 11.2 %collective-permute-start.5 = (f32[256,128]{1,0:T(8,128)S(1)}, f32[256,128]{1,0:T(8,128)S(1)}, u32[]{:S(2)}, u32[]{:S(2)}) collective-permute-start(f32[256,128]{1,0:T(8,128)S(1)} %get-tuple-element.49), channel_id=1, source_target_pairs={{4,0},{8,4},{12,8},{16,12},{20,16},{24,20},{28,24},{32,28},{36,32}... | collective-permute-start | bytes 393224 | tf_op jit(solution)/shard_map/ppermute | solution.py:22
Sparse Core Ops, SparseCore 0:
  46.2 39.4 all-gather.2
  121.8 33.8 all-gather.4
